TPU v7x, 256 devices: a whole 4x4x8 slice. The times are simulated.
256 devices in a mesh: dp: 4 (over y_hi, core), ctx: 64 (over y_lo, z, x).
Axes of the slice: x: 4, y: 4 (y_hi: 2, y_lo: 2; y = y_hi * 2 + y_lo), z: 8, core: 2. Of those that a mesh axis runs over, the one named last changes fastest.
Arguments:
- queries: bfloat16 [4, 4096, 8192], P('dp', None, 'ctx'), may hold values from -6 to 6
- keys_in: bfloat16 [4, 4096, 8192], P('dp', None, 'ctx'), may hold values from -6 to 6
- values_in: bfloat16 [4, 4096, 8192], P('dp', None, 'ctx'), may hold values from -6 to 6
- filters: float32 [256, 128], P(None, 'ctx'), may hold values from -0.6 to 0.6
- grad_out: bfloat16 [4, 4096, 8192], P('dp', None, 'ctx'), may hold values from -6 to 6
Outputs:
- mixed: bfloat16 [4, 4096, 8192], P('dp', None, 'ctx')
- grad_queries: bfloat16 [4, 4096, 8192], P('dp', None, 'ctx')
- grad_keys: bfloat16 [4, 4096, 8192], P('dp', None, 'ctx')
- grad_values: bfloat16 [4, 4096, 8192], P('dp', None, 'ctx')
- grad_filters: float32 [256, 128], P(None, 'ctx')
All inputs are finite; a program needn't handle non-finite values.
Results may differ from a plain program's by a relative error of at most 0.0058.
Values may be sent and summed in bfloat16 or wider, within the bound.
A program may use at most 128 MiB of HBM per device.

v0:
```python
import math

import jax
import jax.numpy as jnp
from jax import lax
from jax.sharding import PartitionSpec as P


def passed_along(block, axis, distance):
    devices = range(lax.axis_size(axis))
    route = [(i - distance, i) for i in devices if i - distance in devices]
    return lax.ppermute(block, axis, route)


def band_half(taps, first):
    width = taps.shape[1]
    padded = jnp.concatenate([taps, jnp.zeros_like(taps)], axis=1)
    rows_at = jnp.arange(width, dtype=jnp.int32)[:, None]
    cols_at = jnp.arange(width, dtype=jnp.int32)[None, :] + first
    offset = rows_at + width - cols_at
    lag_index = jnp.where((offset >= 0) & (offset < width), offset, width)
    return jnp.take(padded, lag_index, axis=1)


def fold_lags(lagged):
    count, width, double = lagged.shape
    flattened = lagged.reshape(count, width * double)
    padded = jnp.pad(flattened, ((0, 0), (0, width)))
    skewed = padded.reshape(count, width, double + 1)
    return jnp.sum(skewed[:, :, 1 : width + 1], axis=1)[:, ::-1]


def local(queries, keys_in, values_in, filters, grad_out):
    taps_all = lax.all_gather(filters.astype(jnp.bfloat16), "ctx", axis=1, tiled=True)
    groups, width = taps_all.shape
    near = band_half(taps_all, 0)
    own = band_half(taps_all, width)
    query_f = queries[0].astype(jnp.float32)
    key_f = keys_in[0].astype(jnp.float32)
    value_f = values_in[0].astype(jnp.float32)
    grad_f = grad_out[0].astype(jnp.float32)
    channels, rows = query_f.shape
    members = channels // groups
    block_count = rows // width

    def blocks(array):
        return array.reshape(groups, members, block_count, width)

    def flat(array):
        return array.reshape(channels, rows)

    product = (key_f * value_f).astype(jnp.bfloat16)
    earlier_rim = passed_along(product, "ctx", 1)
    own_term = jnp.einsum(
        "gim,gsbm->gsbi", own, blocks(product), preferred_element_type=jnp.float32
    )
    earlier = jnp.concatenate([earlier_rim, product[:, : rows - width]], axis=1)
    near_term = jnp.einsum(
        "gim,gsbm->gsbi", near, blocks(earlier), preferred_element_type=jnp.float32
    )
    filtered = flat(own_term + near_term)
    mixed = (query_f * filtered).astype(jnp.bfloat16)
    grad_filtered = (grad_f * query_f).astype(jnp.bfloat16)
    grad_queries = (grad_f * filtered).astype(jnp.bfloat16)
    local_part = jnp.einsum(
        "gim,gsbi->gsbm", own, blocks(grad_filtered), preferred_element_type=jnp.float32
    )
    later_rim = passed_along(grad_filtered, "ctx", -1)
    later = jnp.concatenate([grad_filtered[:, width:], later_rim], axis=1)
    carried = jnp.einsum("gim,gsbi->gsbm", near, blocks(later), preferred_element_type=jnp.float32)
    grad_product = flat(local_part + carried)
    grad_keys = (grad_product * value_f).astype(jnp.bfloat16)
    grad_values = (grad_product * key_f).astype(jnp.bfloat16)
    window = jnp.concatenate([blocks(earlier), blocks(product)], axis=3)
    step_size = math.gcd(groups, 32)
    step_count = groups // step_size

    def lag_block(items):
        grad_part, window_part = items
        lagged = jnp.einsum(
            "gsbi,gsbk->gik", grad_part, window_part, preferred_element_type=jnp.float32
        )
        return fold_lags(lagged)

    grad_blocks = blocks(grad_filtered).reshape(step_count, step_size, members, block_count, width)
    window_blocks = window.reshape(step_count, step_size, members, block_count, 2 * width)
    tap_local = lax.map(lag_block, (grad_blocks, window_blocks)).reshape(groups, width)
    tap_share = lax.psum_scatter(tap_local, "ctx", scatter_dimension=1, tiled=True)
    grad_filters = lax.psum(tap_share, "dp")
    return (mixed[None], grad_queries[None], grad_keys[None], grad_values[None], grad_filters)


def solution(mesh):
    return jax.shard_map(
        local,
        mesh=mesh,
        in_specs=(
            P("dp", None, "ctx"),
            P("dp", None, "ctx"),
            P("dp", None, "ctx"),
            P(None, "ctx"),
            P("dp", None, "ctx"),
        ),
        out_specs=(
            P("dp", None, "ctx"),
            P("dp", None, "ctx"),
            P("dp", None, "ctx"),
            P("dp", None, "ctx"),
            P(None, "ctx"),
        ),
        check_vma=False,
    )
```

profile of v0, /device:TPU:1, one launch (start us, length us, event | category | flops | bytes accessed | tf_op | source)
XLA Modules:
  0.0 1070.8 jit_solution(14008710491644146458)
XLA Ops:
  11.2 143.8 %all-gather = bf16[64,2,256]{2,1,0:T(2,128)(2,1)S(1)} all-gather(bf16[1,2,256]{2,1,0:T(2,128)(2,1)S(1)} %convert_bitcast_fusion), channel_id=1, replica_groups=mesh['dp'=4,'ctx'=64] {'ctx'}, dimensions={0}, use_global_device_ids=true | all-gather | bytes 66560 | tf_op jit(solution)/shard_map/all_gather | solution.py:34
  155.1 65.3 %gather_fusion.1 = bf16[16384,256]{1,0:T(8,128)(2,1)} fusion(bf16[256,256]{0,1:T(8,128)(2,1)S(1)} %concatenate.10, s32[16384]{0:T(1024)S(1)} %get-tuple-element.97), kind=kCustom, calls=%fused_computation.1.clone | custom fusion | bytes 16842752 | tf_op jit(solution)/shard_map/jit(_take)/gather | solution.py:22
  220.4 12.4 %copy.23 = bf16[128,128,256]{1,0,2:T(8,128)(2,1)} copy(bf16[128,128,256]{2,1,0:T(8,128)(2,1)} %bitcast.81) | data formatting | bytes 16777216 | tf_op jit(solution)/shard_map/jit(_take)/gather | solution.py:22
  232.7 65.2 %gather_fusion = bf16[16384,256]{1,0:T(8,128)(2,1)} fusion(bf16[256,256]{0,1:T(8,128)(2,1)S(1)} %concatenate.10, s32[16384]{0:T(1024)S(1)} %get-tuple-element.98), kind=kCustom, calls=%fused_computation.clone | custom fusion | bytes 16842752 | tf_op jit(solution)/shard_map/jit(_take)/gather | solution.py:22
  297.9 12.4 %copy.22 = bf16[128,128,256]{1,0,2:T(8,128)(2,1)} copy(bf16[128,128,256]{2,1,0:T(8,128)(2,1)} %bitcast.80) | data formatting | bytes 16777216 | tf_op jit(solution)/shard_map/jit(_take)/gather | solution.py:22
  310.4 4.8 fusion.10
  320.4 3.7 collective-permute-start
  325.4 9.2 fusion.12
  338.1 142.5 %while.12 = (s32[]{:T(128)}, f32[8,32,128]{2,1,0:T(8,128)}, bf16[8,32,16,1,128]{4,2,1,3,0:T(8,128)(2,1)}, bf16[8,32,16,1,256]{4,2,1,3,0:T(8,128)(2,1)S(1)}, s32[]{:T(128)}, /*index=5*/f32[]{:T(128)}) while((s32[]{:T(128)}, f32[8,32,128]{2,1,0:T(8,128)}, bf16[8,32,16,1,128]{4,2,1,3,0:T(8,128)(2,1)}, bf16[8,32,16,1,256]{4,2,1,3,0:T(8,128)(2,1)S(1)}, ...), condition=%wide.region_2.4_spmd, body=%wide.region_0.0_spmd.sunk | while | flops 34074624 | bytes 31982676 | solution.py:87
  344.5 8.0 reshape.217
  352.5 2.8 slice_reduce_fusion.2
  362.3 8.0 reshape.217
  370.3 2.8 slice_reduce_fusion.2
  380.1 8.0 reshape.217
  388.0 2.8 slice_reduce_fusion.2
  397.9 8.0 reshape.217
  405.8 2.8 slice_reduce_fusion.2
  415.7 8.0 reshape.217
  433.5 8.0 reshape.217
  451.3 8.0 reshape.217
  469.1 8.0 reshape.217
  480.6 8.6 fusion.24
  490.9 527.3 %all-reduce.5.cloned.1.call-done = f32[256,128]{1,0:T(8,128)} async-done(((f32[256,128]{1,0:T(8,128)}), f32[256,128]{1,0:T(8,128)}) %all-reduce.5.cloned.1.call-update) | async-done | bytes 131088
  1019.2 44.1 %psum.7 = f32[256,2]{1,0:T(8,128)S(1)} all-reduce(f32[256,2]{1,0:T(8,128)S(1)} %constant_dynamic-slice_fusion), channel_id=1, replica_groups=mesh['dp'=4,'ctx'=64] {'dp'}, use_global_device_ids=true, to_apply=%region_4.6 | all-reduce | flops 512 | bytes 4096 | tf_op jit(solution)/shard_map/psum | solution.py:89
  (82 shorter events, 84.2 us)
Async XLA Ops:
  7.2 1011.1 %all-reduce.5.cloned.1.call-start = ((), (), s32[]{:S(2)}) async-start(), calls=%async_computation | async-start | bytes 262144
  9.0 301.4 %copy-start.3 = (bf16[1,4096,128]{2,1,0:T(8,128)(2,1)}, bf16[1,4096,128]{2,1,0:T(8,128)(2,1)S(1)}, u32[]{:S(2)}) copy-start(bf16[1,4096,128]{2,1,0:T(8,128)(2,1)S(1)} %fusion.23) | copy-start | bytes 3145732
  9.0 306.2 %collective-permute-start.1 = (bf16[4096,128]{1,0:T(8,128)(2,1)S(1)}, bf16[4096,128]{1,0:T(8,128)(2,1)S(1)}, u32[]{:S(2)}, u32[]{:S(2)}) collective-permute-start(bf16[4096,128]{1,0:T(8,128)(2,1)S(1)} %bitcast.85), channel_id=1, source_target_pairs={{1,0},{2,1},{3,2},{4,3},{5,4},{6,5},{7,6},{8,7},{9,8},{10,9},{11,1... | collective-permute-start | bytes 3145736 | tf_op jit(solution)/shard_map/ppermute | solution.py:12
  310.4 5.8 copy-start
  316.2 2.3 copy-start.4
  316.2 2.3 copy-start.5
  318.5 5.6 copy-start.8
  320.4 15.2 %collective-permute-start = (bf16[4096,128]{1,0:T(8,128)(2,1)S(1)}, bf16[4096,128]{1,0:T(8,128)(2,1)S(1)}, u32[]{:S(2)}, u32[]{:S(2)}) collective-permute-start(bf16[4096,128]{1,0:T(8,128)(2,1)S(1)} %bitcast.82), channel_id=1, source_target_pairs={{0,1},{1,2},{2,3},{3,4},{4,5},{5,6},{6,7},{7,8},{8,9},{9,10},{10,1... | collective-permute-start | bytes 3145736 | tf_op jit(solution)/shard_map/ppermute | solution.py:12
  335.6 1.0 copy-start.6
  338.0 142.5 %copy-start.7 = (bf16[4096,128]{1,0:T(8,128)(2,1)S(1)}, bf16[4096,128]{1,0:T(8,128)(2,1)}, u32[]{:S(2)}) copy-start(bf16[4096,128]{1,0:T(8,128)(2,1)} %copy-done.6) | copy-start | bytes 3145732
  480.5 8.6 copy-start.1
  480.6 8.6 copy-start.2
Sparse Core Ops, SparseCore 0:
  480.7 537.5 all-reduce.4
where the time goes:
time: 1070 us
  waiting for transfers between devices  528 us (49%)
  local copies, waits for them, and re-layouts  266 us (25%)
  blocking collectives  188 us (18%)
  matrix products  38.2 us (4%)
  other arithmetic  30.2 us (3%)
  between operations  14.9 us (1%)
    unnamed x2, waiting for transfers between devices  527 us
    gather x4, local copies, waits for them, and re-layouts, band_half(): return jnp.take(padded, lag_index, axis=1)  155 us
    all_gather x1, blocking collectives, local(): lax.all_gather(filters.astype(jnp.bfloat16), 'ctx', axis=1, tiled=True)  144 us
    reshape x8, local copies, waits for them, and re-layouts, fold_lags(): skewed = padded.reshape(count, width, double + 1)  63.7 us
    psum x1, blocking collectives, local(): grad_filters = lax.psum(tap_share, 'dp')  44.1 us
    reduce_sum x8, other arithmetic, fold_lags(): return jnp.sum(skewed[:, :, 1:width + 1], axis=1)[:, ::-1]  22.4 us
  transfers between devices with their start and end apart: 3, of which 2 were waited for; matrix products, arithmetic and copies ran while one was open for 17% of the time, Pallas kernels for 0%

commit v1 on v0

v1 whole, which is shorter than its diff:
```python
import jax
import jax.numpy as jnp
import ml_dtypes
import numpy as np
from jax import lax
from jax.experimental import pallas as pl
from jax.experimental.pallas import tpu as pltpu
from jax.sharding import PartitionSpec as P

MESH = pl.DeviceIdType.MESH
BF16 = jnp.bfloat16
F32 = jnp.float32

TAPS = 128
WINDOW = 2 * TAPS
MEMBERS = 16
NX, NZ, NYL, NY = 4, 8, 2, 8
LOADS = 8
STEPS = 16


def split(matrix):
    high = matrix.astype(ml_dtypes.bfloat16)
    low = (matrix - high.astype(np.float64)).astype(ml_dtypes.bfloat16)
    return high, low


def transforms():
    k = np.arange(TAPS, dtype=np.float64)
    n = np.arange(WINDOW, dtype=np.float64)
    angle = 2 * np.pi * np.outer(n, k + 0.5) / WINDOW
    forward = np.concatenate([np.cos(angle), -np.sin(angle)], axis=1)
    inverse = np.concatenate([np.cos(angle), -np.sin(angle)], axis=1).T * (2 / WINDOW)
    fh, fl = split(forward)
    into = np.concatenate([fh[:TAPS], fl[:TAPS], fh[TAPS:], fl[TAPS:]], axis=0)
    ih, il = split(inverse)
    late = np.concatenate([ih[:, TAPS:], il[:, TAPS:]], axis=1)
    early = np.concatenate([ih[:, :TAPS], il[:, :TAPS]], axis=1)
    lag = np.arange(TAPS).reshape(NYL, NZ, NX, 2).transpose(1, 0, 2, 3).reshape(-1)
    th, tl = ih[:, lag].T, il[:, lag].T
    tap = np.concatenate([th, tl, th], axis=1)
    return into, np.stack([late, early]), tap


def dot(a, b):
    return jnp.dot(a, b, preferred_element_type=F32)


def two_parts(a):
    high = a.astype(BF16)
    low = (a - high.astype(F32)).astype(BF16)
    return high, low


def mixer_kernel(
    q_h, k_h, v_h, go_h, f_h, into_h, back_h, tap_h,
    mixed, gq, gk, gv, gfilt,
    q, k, v, go, p, gf, prev, nxt, into, back, tap,
    xg, tg, spec, dspec, sa, ra, sb, rb, sc, rc,
    load_sem, const_sem, hs, hr, xs, xr, zs, zr, ys, yr, as_, ar, bs, br, cs, cr,
):
    rows = q.shape[0]
    lrows, srows = rows // LOADS, rows // STEPS
    per_load = lrows // srows
    groups = srows // MEMBERS
    ctx, dp = lax.axis_index("ctx"), lax.axis_index("dp")
    last = NYL * NZ * NX - 1
    x, z, yl = lax.rem(ctx, NX), lax.rem(lax.div(ctx, NX), NZ), lax.div(ctx, NX * NZ)
    y = lax.div(dp, 2) * 4 + yl * 2 + lax.rem(dp, 2)

    def x_peer(d):
        other = lax.rem(x + d, NX)
        return other, {"ctx": ctx - x + other}

    def z_peer(d):
        other = lax.rem(z + d, NZ)
        return other, {"ctx": ctx + (other - z) * NX}

    def y_peer(d):
        t = lax.rem(y + d, NY)
        its_yl = lax.rem(lax.div(t, 2), 2)
        return its_yl, {
            "dp": lax.div(t, 4) * 2 + lax.rem(t, 2),
            "ctx": ctx + (its_yl - yl) * (NX * NZ),
        }

    right = {"ctx": lax.rem(ctx + 1, last + 1)}
    left = {"ctx": lax.rem(ctx + last, last + 1)}
    other_half = {"ctx": ctx + (1 - 2 * yl) * (NX * NZ)}

    def load(which, i):
        src, dst = ((k_h, k), (v_h, v), (q_h, q), (go_h, go))[which]
        at = pl.ds(pl.multiple_of(i * lrows, lrows), lrows)
        return pltpu.make_async_copy(src.at[at], dst.at[at], load_sem.at[which, i])

    taps_load = pltpu.make_async_copy(f_h, xg.at[x], const_sem.at[0])
    taps_load.start()
    for i in range(LOADS):
        load(0, i).start()
        load(1, i).start()
        load(2, LOADS - 1 - i).start()
        load(3, LOADS - 1 - i).start()
    consts = [
        pltpu.make_async_copy(src, dst, const_sem.at[1 + n])
        for n, (src, dst) in enumerate(((into_h, into), (back_h, back), (tap_h, tap)))
    ]
    for c in consts:
        c.start()

    barrier = pltpu.get_barrier_semaphore()
    greeted = [right, left]
    greeted += [x_peer(d)[1] for d in range(1, NX)]
    greeted += [z_peer(d)[1] for d in range(1, NZ)]
    greeted += [y_peer(d)[1] for d in range(1, NY)]
    for device in greeted:
        pl.semaphore_signal(barrier, inc=1, device_id=device, device_id_type=MESH)

    def at_step(i):
        return pl.ds(pl.multiple_of(i * srows, srows), srows)

    def send_p(i):
        return pltpu.make_async_remote_copy(
            src_ref=p.at[at_step(i)], dst_ref=prev.at[at_step(i)],
            send_sem=hs.at[0, i], recv_sem=hr.at[0, i],
            device_id=right, device_id_type=MESH,
        )

    def send_gf(i):
        return pltpu.make_async_remote_copy(
            src_ref=gf.at[at_step(i)], dst_ref=nxt.at[at_step(i)],
            send_sem=hs.at[1, i], recv_sem=hr.at[1, i],
            device_id=left, device_id_type=MESH,
        )

    def products(i):
        j = LOADS - 1 - i
        load(0, i).wait()
        load(1, i).wait()
        at = pl.ds(pl.multiple_of(i * lrows, lrows), lrows)
        p[at, :] = (k[at, :].astype(F32) * v[at, :].astype(F32)).astype(BF16)
        load(2, j).wait()
        load(3, j).wait()
        at = pl.ds(pl.multiple_of(j * lrows, lrows), lrows)
        gf[at, :] = (q[at, :].astype(F32) * go[at, :].astype(F32)).astype(BF16)

    def send(i):
        for s in range(per_load):
            n = i * per_load + s

            @pl.when(ctx < last)
            def _():
                send_p(n).start()

            @pl.when(ctx > 0)
            def _():
                send_gf(STEPS - 1 - n).start()

    products(0)
    taps_load.wait()
    pl.semaphore_wait(barrier, len(greeted))

    gather_x = [
        pltpu.make_async_remote_copy(
            src_ref=xg.at[x], dst_ref=xg.at[x],
            send_sem=xs.at[d - 1], recv_sem=xr.at[d - 1],
            device_id=x_peer(d)[1], device_id_type=MESH,
        )
        for d in range(1, NX)
    ]
    for c in gather_x:
        c.start()
    send(0)

    @pl.loop(1, LOADS)
    def _(i):
        products(i)
        send(i)

    @pl.when(ctx == 0)
    def _():
        prev[...] = jnp.zeros_like(prev)

    @pl.when(ctx == last)
    def _():
        nxt[...] = jnp.zeros_like(nxt)

    for c in gather_x:
        c.wait()
    mine = jnp.concatenate([xg[i] for i in range(NX)], axis=0)
    tg[yl, z] = mine.astype(BF16).astype(F32)
    gather_z = [
        pltpu.make_async_remote_copy(
            src_ref=tg.at[yl, z], dst_ref=tg.at[yl, z],
            send_sem=zs.at[d - 1], recv_sem=zr.at[d - 1],
            device_id=z_peer(d)[1], device_id_type=MESH,
        )
        for d in range(1, NZ)
    ]
    for c in gather_z:
        c.start()
    for c in gather_z:
        c.wait()
    gather_y = pltpu.make_async_remote_copy(
        src_ref=tg.at[yl], dst_ref=tg.at[yl], send_sem=ys, recv_sem=yr,
        device_id=other_half, device_id_type=MESH,
    )
    gather_y.start()
    for c in consts:
        c.wait()
    gather_y.wait()
    taps = tg[...].reshape(TAPS, -1).T.astype(BF16)
    spec[...] = dot(jnp.concatenate([taps, taps], axis=1), into[:WINDOW, :])

    def spectrum_at(i):
        at = pl.ds(pl.multiple_of(i * groups, groups), groups)

        def spread(a):
            return jnp.broadcast_to(a[:, None, :], (groups, MEMBERS, TAPS)).reshape(srows, TAPS)

        return spread(spec[at, :TAPS]), spread(spec[at, TAPS:])

    def positions(re, im, which):
        high, low = two_parts(jnp.concatenate([re, im], axis=1))
        both = dot(high, back[which])
        return both[:, :TAPS] + both[:, TAPS:] + dot(low, back[which, :, :TAPS])

    def tap_products(i, gre, gim, pre, pim):
        def total(a):
            return jnp.sum(a.reshape(groups, MEMBERS, TAPS), axis=1)

        at = pl.ds(pl.multiple_of(i * groups, groups), groups)
        dspec[at, :TAPS] = total(gre * pre + gim * pim)
        dspec[at, TAPS:] = total(gim * pre - gre * pim)

    def forward_step(i, with_taps):
        @pl.when(ctx > 0)
        def _():
            send_p(i).wait_recv()

        at = at_step(i)
        before, own = prev[at, :], p[at, :]
        window = dot(jnp.concatenate([before, before, own, own], axis=1), into[...])
        re, im = window[:, :TAPS], window[:, TAPS:]
        hre, him = spectrum_at(i)
        filtered = positions(re * hre - im * him, re * him + im * hre, 0)
        mixed[at, :] = (q[at, :].astype(F32) * filtered).astype(BF16)
        gq[at, :] = (go[at, :].astype(F32) * filtered).astype(BF16)
        if with_taps:
            g = gf[at, :]
            gw = dot(jnp.concatenate([g, g], axis=1), into[WINDOW:, :])
            tap_products(i, gw[:, :TAPS], gw[:, TAPS:], re, im)

    def backward_step(i, with_taps):
        @pl.when(ctx < last)
        def _():
            send_gf(i).wait_recv()

        at = at_step(i)
        own, after = gf[at, :], nxt[at, :]
        window = dot(jnp.concatenate([own, own, after, after], axis=1), into[...])
        re, im = window[:, :TAPS], window[:, TAPS:]
        hre, him = spectrum_at(i)
        grad = positions(re * hre + im * him, im * hre - re * him, 1)
        gk[at, :] = (v[at, :].astype(F32) * grad).astype(BF16)
        gv[at, :] = (k[at, :].astype(F32) * grad).astype(BF16)
        if with_taps:
            b = p[at, :]
            pw = dot(jnp.concatenate([b, b], axis=1), into[:WINDOW, :])
            tap_products(i, re, im, pw[:, :TAPS], pw[:, TAPS:])

    def steps(start, stop, with_taps):
        @pl.loop(start, stop)
        def _(i):
            forward_step(i, with_taps)
            backward_step(STEPS - 1 - i, with_taps)

    steps(0, STEPS // 2, True)

    high, low = two_parts(dspec[...])
    grads = lax.dot_general(
        tap[...], jnp.concatenate([high, high, low], axis=1),
        (((1,), (1,)), ((), ())), preferred_element_type=F32,
    )
    sa[...] = grads.reshape(sa.shape)
    ra[z] = sa[z]
    reduce_z = []
    for d in range(1, NZ):
        other, device = z_peer(d)
        reduce_z.append(
            pltpu.make_async_remote_copy(
                src_ref=sa.at[other], dst_ref=ra.at[z],
                send_sem=as_.at[d - 1], recv_sem=ar.at[d - 1],
                device_id=device, device_id_type=MESH,
            )
        )
    for c in reduce_z:
        c.start()

    steps(STEPS // 2, 11, False)

    for c in reduce_z:
        c.wait()
    sb[...] = jnp.sum(ra[...], axis=0).reshape(sb.shape)
    rb[y] = sb[yl]
    reduce_y = []
    for d in range(1, NY):
        its_yl, device = y_peer(d)
        reduce_y.append(
            pltpu.make_async_remote_copy(
                src_ref=sb.at[its_yl], dst_ref=rb.at[y],
                send_sem=bs.at[d - 1], recv_sem=br.at[d - 1],
                device_id=device, device_id_type=MESH,
            )
        )
    for c in reduce_y:
        c.start()

    steps(11, 13, False)

    for c in reduce_y:
        c.wait()
    part = jnp.sum(rb[...], axis=0)
    for i in range(NX):
        sc[i] = part[2 * i : 2 * i + 2]
    rc[x] = sc[x]
    reduce_x = []
    for d in range(1, NX):
        other, device = x_peer(d)
        reduce_x.append(
            pltpu.make_async_remote_copy(
                src_ref=sc.at[other], dst_ref=rc.at[x],
                send_sem=cs.at[d - 1], recv_sem=cr.at[d - 1],
                device_id=device, device_id_type=MESH,
            )
        )
    for c in reduce_x:
        c.start()

    steps(13, STEPS, False)

    for c in reduce_x:
        c.wait()
    gfilt[...] = jnp.sum(rc[...], axis=0)

    @pl.loop(0, STEPS)
    def _(i):
        @pl.when(ctx < last)
        def _():
            send_p(i).wait_send()

        @pl.when(ctx > 0)
        def _():
            send_gf(i).wait_send()


def write_kernel(*refs):
    count = len(refs) // 2
    sems = refs[-1]
    copies = [
        pltpu.make_async_copy(refs[i], refs[count + i], sems.at[i]) for i in range(count)
    ]
    for c in copies:
        c.start()
    for c in copies:
        c.wait()


def local(queries, keys_in, values_in, filters, grad_out):
    rows, width = queries.shape[1:]
    groups = filters.shape[0]
    into, back, tap = (jnp.asarray(m) for m in transforms())
    slab = (rows, width)
    dma = pltpu.SemaphoreType.DMA
    anywhere = pl.BlockSpec(memory_space=pl.ANY)
    in_vmem = pl.BlockSpec(memory_space=pltpu.VMEM)
    operands = [queries[0], keys_in[0], values_in[0], grad_out[0], filters.T, into, back, tap]
    operands = [pltpu.with_memory_space_constraint(a, pltpu.HBM) for a in operands]
    outs = pl.pallas_call(
        mixer_kernel,
        out_shape=[pltpu.VMEM(slab, BF16)] * 4 + [pltpu.VMEM((2, groups), F32)],
        in_specs=[anywhere] * len(operands),
        out_specs=[in_vmem] * 5,
        scratch_shapes=[
            *[pltpu.VMEM(slab, BF16)] * 8,
            pltpu.VMEM(into.shape, BF16), pltpu.VMEM(back.shape, BF16), pltpu.VMEM(tap.shape, BF16),
            pltpu.VMEM((NX, 2, groups), F32), pltpu.VMEM((NYL, NZ, 2 * NX, groups), F32),
            pltpu.VMEM((groups, WINDOW), F32), pltpu.VMEM((groups, WINDOW), F32),
            pltpu.VMEM((NZ, 16, groups), F32), pltpu.VMEM((NZ, 16, groups), F32),
            pltpu.VMEM((NYL, 8, groups), F32), pltpu.VMEM((NY, 8, groups), F32),
            pltpu.VMEM((NX, 2, groups), F32), pltpu.VMEM((NX, 2, groups), F32),
            dma((4, LOADS)), dma((4,)), dma((2, STEPS)), dma((2, STEPS)),
            dma((NX - 1,)), dma((NX - 1,)), dma((NZ - 1,)), dma((NZ - 1,)), dma, dma,
            dma((NZ - 1,)), dma((NZ - 1,)), dma((NY - 1,)), dma((NY - 1,)),
            dma((NX - 1,)), dma((NX - 1,)),
        ],
        compiler_params=pltpu.CompilerParams(
            collective_id=0, has_side_effects=True, vmem_limit_bytes=40 * 2**20
        ),
        name="mixer",
    )(*operands)
    outs = [pltpu.with_memory_space_constraint(a, pltpu.VMEM) for a in outs]
    written = pl.pallas_call(
        write_kernel,
        out_shape=[pltpu.HBM(a.shape, a.dtype) for a in outs],
        in_specs=[anywhere] * 5,
        out_specs=[anywhere] * 5,
        scratch_shapes=[dma((5,))],
        compiler_params=pltpu.CompilerParams(vmem_limit_bytes=2**20),
        name="write",
    )(*outs)
    return (*[a[None] for a in written[:4]], written[4].T)


def solution(mesh):
    return jax.shard_map(
        local,
        mesh=mesh,
        in_specs=(
            P("dp", None, "ctx"),
            P("dp", None, "ctx"),
            P("dp", None, "ctx"),
            P(None, "ctx"),
            P("dp", None, "ctx"),
        ),
        out_specs=(
            P("dp", None, "ctx"),
            P("dp", None, "ctx"),
            P("dp", None, "ctx"),
            P("dp", None, "ctx"),
            P(None, "ctx"),
        ),
        check_vma=False,
    )
```

time: 1070 us -> 66.1 us (0.06)
  waiting for transfers between devices: 528 us -> 0 us
  local copies, waits for them, and re-layouts: 266 us -> 0 us
  blocking collectives: 188 us -> 0 us
  Pallas kernels: 0 us -> 65.3 us
  matrix products: 38.2 us -> 0 us
  other arithmetic: 30.2 us -> 0 us
  between operations: 14.9 us -> 0.64 us
    unnamed x2 -> x0, waiting for transfers between devices: 527 us -> none
    gather x4 -> x0, local copies, waits for them, and re-layouts: 155 us -> none  [band_half(): return jnp.take(padded, lag_index, axis=1)]
    all_gather x1 -> x0, blocking collectives: 144 us -> none  [local(): lax.all_gather(filters.astype(jnp.bfloat16), 'ctx', axis=1, tiled=True)]
    pallas_call x0 -> x2, Pallas kernels: none -> 65.3 us  [the longest x1 63.3 us: local(): pl.pallas_call(mixer_kernel, out_shape=[pltpu.VMEM(slab, BF16)] * 4 + [pl...]
    reshape x8 -> x0, local copies, waits for them, and re-layouts: 63.7 us -> none  [fold_lags(): skewed = padded.reshape(count, width, double + 1)]
    psum x1 -> x0, blocking collectives: 44.1 us -> none  [local(): grad_filters = lax.psum(tap_share, 'dp')]
    dot_general x12 -> x0, matrix products: 38.2 us -> none  [the longest x8 13.3 us: lag_block(): jnp.einsum('gsbi,gsbk->gik', grad_part, window_part, preferred_element_ty...]
    reduce_sum x8 -> x0, other arithmetic: 22.4 us -> none  [fold_lags(): return jnp.sum(skewed[:, :, 1:width + 1], axis=1)[:, ::-1]]
  transfers between devices with their start and end apart: 3 -> 0, of which waited for: 2 -> 0; matrix products, arithmetic and copies ran while one was open for 17% -> 0% of each run, Pallas kernels for 0% -> 0%
where the time goes in v1:
time: 66.1 us; the launch traced here: 66 us
  Pallas kernels  65.3 us (99%)
    pallas_call x1, Pallas kernels, local(): pl.pallas_call(mixer_kernel, out_shape=[pltpu.VMEM(slab, BF16)] * 4 + [pl...  63.3 us
    pallas_call x1, Pallas kernels, local(): pl.pallas_call(write_kernel, out_shape=[pltpu.HBM(a.shape, a.dtype) for a...  2.05 us

profile of v1, /device:TPU:1, one launch (start us, length us, event | category | flops | bytes accessed | tf_op | source)
XLA Modules:
  0.0 66.0 jit_solution(12834843736901318768)
XLA Ops:
  0.6 63.3 %mixer.1 = (bf16[4096,128]{1,0:T(8,128)(2,1)S(1)}, bf16[4096,128]{1,0:T(8,128)(2,1)S(1)}, bf16[4096,128]{1,0:T(8,128)(2,1)S(1)}, bf16[4096,128]{1,0:T(8,128)(2,1)S(1)}, f32[2,256]{1,0:T(2,128)S(1)}) custom-call(bf16[4096,128]{1,0:T(8,128)(2,1)} %bitcast.10, bf16[4096,128]{1,0:T(8,128)(2,1)} %bitcast.11, bf16[4096,128]{1,0:T(8,128)(2,1)} %bitcast.12, ...), custom_call_target="tpu_custom_call" | custom-call | tf_op jit(solution)/shard_map/mixer/pallas_call | solution.py:378
  63.9 2.1 %write.1 = (bf16[4096,128]{1,0:T(8,128)(2,1)}, bf16[4096,128]{1,0:T(8,128)(2,1)}, bf16[4096,128]{1,0:T(8,128)(2,1)}, bf16[4096,128]{1,0:T(8,128)(2,1)}, f32[2,256]{1,0:T(2,128)}) custom-call(bf16[4096,128]{1,0:T(8,128)(2,1)S(1)} %get-tuple-element.15.refs_0_, bf16[4096,128]{1,0:T(8,128)(2,1)S(1)} %get-tuple-element.16.refs_1_, ...), custom_call_target="tpu_custom_call" | custom-call | tf_op jit(solution)/shard_map/write/pallas_call | solution.py:402

commit v2 on v1

--- a/solution.py
+++ b/solution.py
@@ -17,6 +17,7 @@
 NX, NZ, NYL, NY = 4, 8, 2, 8
 LOADS = 8
 STEPS = 16
+AHEAD, LATER, DEEP = 8, 2, 4
 
 
 def split(matrix):
@@ -56,7 +57,7 @@
     q_h, k_h, v_h, go_h, f_h, into_h, back_h, tap_h,
     mixed, gq, gk, gv, gfilt,
     q, k, v, go, p, gf, prev, nxt, into, back, tap,
-    xg, tg, spec, dspec, sa, ra, sb, rb, sc, rc,
+    xg, zg, spec, dspec, fspec, bspec, sa, ra, sb, rb, sc, rc,
     load_sem, const_sem, hs, hr, xs, xr, zs, zr, ys, yr, as_, ar, bs, br, cs, cr,
 ):
     rows = q.shape[0]
@@ -76,17 +77,33 @@
         other = lax.rem(z + d, NZ)
         return other, {"ctx": ctx + (other - z) * NX}
 
-    def y_peer(d):
-        t = lax.rem(y + d, NY)
-        its_yl = lax.rem(lax.div(t, 2), 2)
-        return its_yl, {
-            "dp": lax.div(t, 4) * 2 + lax.rem(t, 2),
-            "ctx": ctx + (its_yl - yl) * (NX * NZ),
-        }
+    def beside_peer(d):
+        other = lax.rem(z + d, NZ)
+        return {"ctx": ctx + (other - z) * NX + 1 - 2 * lax.rem(x, 2)}
 
     right = {"ctx": lax.rem(ctx + 1, last + 1)}
     left = {"ctx": lax.rem(ctx + last, last + 1)}
-    other_half = {"ctx": ctx + (1 - 2 * yl) * (NX * NZ)}
+    half = NX * NZ
+    other_half = {"ctx": ctx + (1 - 2 * yl) * half}
+    unable = (ctx == 0) | (ctx == last)
+    from_low, to_low = half - NX, half + NX - 1
+    helper = (ctx == from_low) | (ctx == to_low)
+    helped = (ctx == half) | (ctx == half - 1)
+    helper_pair = {"ctx": jnp.where(ctx == from_low, half, jnp.where(ctx == half, from_low, jnp.where(ctx == to_low, half - 1, to_low)))}
+    aside = 1 - 2 * lax.div(x, 2)
+
+    def turn_z(amount):
+        return lax.rem(z + amount + NZ, NZ)
+
+    def sum_y_peer(t, amount):
+        its_yl = (t // 2) % 2
+        return its_yl, {
+            "dp": (t // 4) * 2 + t % 2,
+            "ctx": ctx + (its_yl - yl) * half + (turn_z(amount) - z) * NX,
+        }
+
+    def sum_x_peer(t, amount):
+        return {"ctx": ctx + t - x + (turn_z(amount) - z) * NX}
 
     def load(which, i):
         src, dst = ((k_h, k), (v_h, v), (q_h, q), (go_h, go))[which]
@@ -108,12 +125,27 @@
         c.start()
 
     barrier = pltpu.get_barrier_semaphore()
+    middle = (x == 1) | (x == 2)
     greeted = [right, left]
     greeted += [x_peer(d)[1] for d in range(1, NX)]
     greeted += [z_peer(d)[1] for d in range(1, NZ)]
-    greeted += [y_peer(d)[1] for d in range(1, NY)]
+    greeted += [sum_y_peer(t, -aside)[1] for t in range(NY)]
+    greeted += [sum_x_peer(t, 2 * (t // 2) - 1) for t in range(NX)]
     for device in greeted:
         pl.semaphore_signal(barrier, inc=1, device_id=device, device_id_type=MESH)
+
+    @pl.when(jnp.logical_not(middle))
+    def _():
+        for d in range(1, NZ):
+            pl.semaphore_signal(barrier, inc=1, device_id=beside_peer(d), device_id_type=MESH)
+
+    @pl.when(jnp.logical_not(helped))
+    def _():
+        pl.semaphore_signal(barrier, inc=1, device_id=other_half, device_id_type=MESH)
+
+    @pl.when(helped)
+    def _():
+        pl.semaphore_signal(barrier, inc=1, device_id=helper_pair, device_id_type=MESH)
 
     def at_step(i):
         return pl.ds(pl.multiple_of(i * srows, srows), srows)
@@ -143,21 +175,10 @@
         at = pl.ds(pl.multiple_of(j * lrows, lrows), lrows)
         gf[at, :] = (q[at, :].astype(F32) * go[at, :].astype(F32)).astype(BF16)
 
-    def send(i):
-        for s in range(per_load):
-            n = i * per_load + s
-
-            @pl.when(ctx < last)
-            def _():
-                send_p(n).start()
-
-            @pl.when(ctx > 0)
-            def _():
-                send_gf(STEPS - 1 - n).start()
-
     products(0)
     taps_load.wait()
-    pl.semaphore_wait(barrier, len(greeted))
+    count = len(greeted) + jnp.where(middle, NZ - 1, 0) + jnp.where(unable, 0, 1) + jnp.where(helper, 1, 0)
+    pl.semaphore_wait(barrier, count)
 
     gather_x = [
         pltpu.make_async_remote_copy(
@@ -167,14 +188,84 @@
         )
         for d in range(1, NX)
     ]
+    gather_z = [
+        [
+            pltpu.make_async_remote_copy(
+                src_ref=zg.at[yl, z], dst_ref=zg.at[yl, z],
+                send_sem=zs.at[n, d - 1], recv_sem=zr.at[d - 1],
+                device_id=device, device_id_type=MESH,
+            )
+            for n, device in enumerate((z_peer(d)[1], beside_peer(d)))
+        ]
+        for d in range(1, NZ)
+    ]
+    gather_y, gather_help = (
+        pltpu.make_async_remote_copy(
+            src_ref=zg.at[yl], dst_ref=zg.at[yl], send_sem=ys.at[n], recv_sem=yr,
+            device_id=device, device_id_type=MESH,
+        )
+        for n, device in enumerate((other_half, helper_pair))
+    )
+    reduce_z, reduce_y, reduce_x = [], [], []
+    for d in range(1, NZ):
+        other, device = z_peer(d)
+        reduce_z.append(
+            pltpu.make_async_remote_copy(
+                src_ref=sa.at[lax.rem(other + 2 * aside + NZ, NZ)], dst_ref=ra.at[z],
+                send_sem=as_.at[d - 1], recv_sem=ar.at[d - 1],
+                device_id=device, device_id_type=MESH,
+            )
+        )
+    for t in range(NY):
+        its_yl, device = sum_y_peer(t, aside)
+        reduce_y.append(
+            pltpu.make_async_remote_copy(
+                src_ref=sb.at[its_yl], dst_ref=rb.at[y],
+                send_sem=bs.at[t], recv_sem=br.at[y],
+                device_id=device, device_id_type=MESH,
+            )
+        )
+    for t in range(NX):
+        reduce_x.append(
+            pltpu.make_async_remote_copy(
+                src_ref=sc.at[t], dst_ref=rc.at[x],
+                send_sem=cs.at[t], recv_sem=cr.at[x],
+                device_id=sum_x_peer(t, aside), device_id_type=MESH,
+            )
+        )
+
+    def wait_sum(copies, landed, recv_sems):
+        for n, c in enumerate(copies):
+            c.wait_send()
+            pltpu.make_async_remote_copy(
+                src_ref=landed.at[n], dst_ref=landed.at[n],
+                send_sem=recv_sems.at[n], recv_sem=recv_sems.at[n],
+                device_id=right, device_id_type=MESH,
+            ).wait_recv()
+
     for c in gather_x:
         c.start()
-    send(0)
+
+    def send(n):
+        @pl.when(ctx < last)
+        def _():
+            send_p(n).start()
+
+        @pl.when(ctx > 0)
+        def _():
+            send_gf(STEPS - 1 - n).start()
+
+    for s in range(per_load):
+        send(s)
 
     @pl.loop(1, LOADS)
     def _(i):
         products(i)
-        send(i)
+
+        @pl.when(i * per_load < AHEAD)
+        def _():
+            for s in range(per_load):
+                send(i * per_load + s)
 
     @pl.when(ctx == 0)
     def _():
@@ -184,97 +275,100 @@
     def _():
         nxt[...] = jnp.zeros_like(nxt)
 
+    for c in consts:
+        c.wait()
     for c in gather_x:
         c.wait()
     mine = jnp.concatenate([xg[i] for i in range(NX)], axis=0)
-    tg[yl, z] = mine.astype(BF16).astype(F32)
-    gather_z = [
-        pltpu.make_async_remote_copy(
-            src_ref=tg.at[yl, z], dst_ref=tg.at[yl, z],
-            send_sem=zs.at[d - 1], recv_sem=zr.at[d - 1],
-            device_id=z_peer(d)[1], device_id_type=MESH,
-        )
-        for d in range(1, NZ)
-    ]
-    for c in gather_z:
-        c.start()
-    for c in gather_z:
-        c.wait()
-    gather_y = pltpu.make_async_remote_copy(
-        src_ref=tg.at[yl], dst_ref=tg.at[yl], send_sem=ys, recv_sem=yr,
-        device_id=other_half, device_id_type=MESH,
-    )
-    gather_y.start()
-    for c in consts:
-        c.wait()
-    gather_y.wait()
-    taps = tg[...].reshape(TAPS, -1).T.astype(BF16)
-    spec[...] = dot(jnp.concatenate([taps, taps], axis=1), into[:WINDOW, :])
-
-    def spectrum_at(i):
-        at = pl.ds(pl.multiple_of(i * groups, groups), groups)
-
-        def spread(a):
-            return jnp.broadcast_to(a[:, None, :], (groups, MEMBERS, TAPS)).reshape(srows, TAPS)
-
-        return spread(spec[at, :TAPS]), spread(spec[at, TAPS:])
+    zg[yl, z] = jnp.concatenate([mine[:, :TAPS], mine[:, TAPS:]], axis=0).astype(BF16)
+
+    @pl.when(middle)
+    def _():
+        for pair in gather_z:
+            for c in pair:
+                c.start()
+
+    def spread(a):
+        return jnp.broadcast_to(a[:, None, :], (groups, MEMBERS, TAPS)).reshape(srows, TAPS)
+
+    def group_rows(i):
+        return pl.ds(pl.multiple_of(i * groups, groups), groups)
 
     def positions(re, im, which):
         high, low = two_parts(jnp.concatenate([re, im], axis=1))
         both = dot(high, back[which])
         return both[:, :TAPS] + both[:, TAPS:] + dot(low, back[which, :, :TAPS])
 
-    def tap_products(i, gre, gim, pre, pim):
-        def total(a):
-            return jnp.sum(a.reshape(groups, MEMBERS, TAPS), axis=1)
-
-        at = pl.ds(pl.multiple_of(i * groups, groups), groups)
-        dspec[at, :TAPS] = total(gre * pre + gim * pim)
-        dspec[at, TAPS:] = total(gim * pre - gre * pim)
-
-    def forward_step(i, with_taps):
+    def arrived(i):
         @pl.when(ctx > 0)
         def _():
             send_p(i).wait_recv()
 
+        @pl.when(ctx < last)
+        def _():
+            send_gf(STEPS - 1 - i).wait_recv()
+
+    def forward_window(i):
+        before, own = prev[at_step(i), :], p[at_step(i), :]
+        return dot(jnp.concatenate([before, before, own, own], axis=1), into[...])
+
+    def backward_window(i):
+        own, after = gf[at_step(i), :], nxt[at_step(i), :]
+        return dot(jnp.concatenate([own, own, after, after], axis=1), into[...])
+
+    def forward_outputs(i, window):
         at = at_step(i)
-        before, own = prev[at, :], p[at, :]
-        window = dot(jnp.concatenate([before, before, own, own], axis=1), into[...])
         re, im = window[:, :TAPS], window[:, TAPS:]
-        hre, him = spectrum_at(i)
+        hre, him = spread(spec[group_rows(i), :TAPS]), spread(spec[group_rows(i), TAPS:])
         filtered = positions(re * hre - im * him, re * him + im * hre, 0)
         mixed[at, :] = (q[at, :].astype(F32) * filtered).astype(BF16)
         gq[at, :] = (go[at, :].astype(F32) * filtered).astype(BF16)
-        if with_taps:
-            g = gf[at, :]
-            gw = dot(jnp.concatenate([g, g], axis=1), into[WINDOW:, :])
-            tap_products(i, gw[:, :TAPS], gw[:, TAPS:], re, im)
-
-    def backward_step(i, with_taps):
-        @pl.when(ctx < last)
-        def _():
-            send_gf(i).wait_recv()
-
+
+    def backward_outputs(i, window):
         at = at_step(i)
-        own, after = gf[at, :], nxt[at, :]
-        window = dot(jnp.concatenate([own, own, after, after], axis=1), into[...])
         re, im = window[:, :TAPS], window[:, TAPS:]
-        hre, him = spectrum_at(i)
+        hre, him = spread(spec[group_rows(i), :TAPS]), spread(spec[group_rows(i), TAPS:])
         grad = positions(re * hre + im * him, im * hre - re * him, 1)
         gk[at, :] = (v[at, :].astype(F32) * grad).astype(BF16)
         gv[at, :] = (k[at, :].astype(F32) * grad).astype(BF16)
-        if with_taps:
-            b = p[at, :]
-            pw = dot(jnp.concatenate([b, b], axis=1), into[:WINDOW, :])
-            tap_products(i, re, im, pw[:, :TAPS], pw[:, TAPS:])
-
-    def steps(start, stop, with_taps):
-        @pl.loop(start, stop)
-        def _(i):
-            forward_step(i, with_taps)
-            backward_step(STEPS - 1 - i, with_taps)
-
-    steps(0, STEPS // 2, True)
+
+    def tap_products(i, g, b):
+        def total(a):
+            return jnp.sum(a.reshape(groups, MEMBERS, TAPS), axis=1)
+
+        gre, gim, bre, bim = g[:, :TAPS], g[:, TAPS:], b[:, :TAPS], b[:, TAPS:]
+        dspec[group_rows(i), :TAPS] = total(gre * bre + gim * bim)
+        dspec[group_rows(i), TAPS:] = total(gim * bre - gre * bim)
+
+    @pl.loop(0, STEPS // 2)
+    def _(i):
+        @pl.when(i + AHEAD < STEPS // 2 + LATER)
+        def _():
+            send(i + AHEAD)
+
+        arrived(i)
+        j = STEPS - 1 - i
+        fw, bw = forward_window(i), backward_window(j)
+        g, b = gf[at_step(i), :], p[at_step(j), :]
+        gw = dot(jnp.concatenate([g, g], axis=1), into[WINDOW:, :])
+        bp = dot(jnp.concatenate([b, b], axis=1), into[:WINDOW, :])
+        tap_products(i, gw, fw)
+        tap_products(j, bw, bp)
+        fspec[at_step(i), :] = fw
+        bspec[at_step(i), :] = bw
+
+        @pl.when(i == 2)
+        def _():
+            for pair in gather_z:
+                pair[0].wait_recv()
+
+            @pl.when(jnp.logical_not(unable))
+            def _():
+                gather_y.start()
+
+            @pl.when(helper)
+            def _():
+                gather_help.start()
 
     high, low = two_parts(dspec[...])
     grads = lax.dot_general(
@@ -282,64 +376,63 @@
         (((1,), (1,)), ((), ())), preferred_element_type=F32,
     )
     sa[...] = grads.reshape(sa.shape)
-    ra[z] = sa[z]
-    reduce_z = []
-    for d in range(1, NZ):
-        other, device = z_peer(d)
-        reduce_z.append(
-            pltpu.make_async_remote_copy(
-                src_ref=sa.at[other], dst_ref=ra.at[z],
-                send_sem=as_.at[d - 1], recv_sem=ar.at[d - 1],
-                device_id=device, device_id_type=MESH,
-            )
-        )
+    ra[z] = sa[turn_z(2 * aside)]
     for c in reduce_z:
         c.start()
-
-    steps(STEPS // 2, 11, False)
-
-    for c in reduce_z:
-        c.wait()
-    sb[...] = jnp.sum(ra[...], axis=0).reshape(sb.shape)
-    rb[y] = sb[yl]
-    reduce_y = []
-    for d in range(1, NY):
-        its_yl, device = y_peer(d)
-        reduce_y.append(
-            pltpu.make_async_remote_copy(
-                src_ref=sb.at[its_yl], dst_ref=rb.at[y],
-                send_sem=bs.at[d - 1], recv_sem=br.at[d - 1],
-                device_id=device, device_id_type=MESH,
-            )
-        )
-    for c in reduce_y:
-        c.start()
-
-    steps(11, 13, False)
-
-    for c in reduce_y:
-        c.wait()
-    part = jnp.sum(rb[...], axis=0)
-    for i in range(NX):
-        sc[i] = part[2 * i : 2 * i + 2]
-    rc[x] = sc[x]
-    reduce_x = []
-    for d in range(1, NX):
-        other, device = x_peer(d)
-        reduce_x.append(
-            pltpu.make_async_remote_copy(
-                src_ref=sc.at[other], dst_ref=rc.at[x],
-                send_sem=cs.at[d - 1], recv_sem=cr.at[d - 1],
-                device_id=device, device_id_type=MESH,
-            )
-        )
-    for c in reduce_x:
-        c.start()
-
-    steps(13, STEPS, False)
-
-    for c in reduce_x:
-        c.wait()
+    for n in range(LATER, DEEP):
+        send(STEPS // 2 + n)
+
+    gather_y.wait_recv()
+
+    @pl.when(jnp.logical_not(unable))
+    def _():
+        gather_y.wait_send()
+
+    @pl.when(helper)
+    def _():
+        gather_help.wait_send()
+
+    @pl.when(middle)
+    def _():
+        for pair in gather_z:
+            for c in pair:
+                c.wait_send()
+
+    tiles = [zg[a, b].astype(F32) for a in range(NYL) for b in range(NZ)]
+    taps = jnp.concatenate([jnp.concatenate([t[:8], t[8:]], axis=1) for t in tiles], axis=0).T.astype(BF16)
+    spec[...] = dot(jnp.concatenate([taps, taps], axis=1), into[:WINDOW, :])
+
+    @pl.loop(STEPS // 2, STEPS)
+    def _(i):
+        @pl.when(i + DEEP < STEPS)
+        def _():
+            send(i + DEEP)
+
+        old = i - STEPS // 2
+        forward_outputs(old, fspec[at_step(old), :])
+        backward_outputs(STEPS - 1 - old, bspec[at_step(old), :])
+        arrived(i)
+        forward_outputs(i, forward_window(i))
+        backward_outputs(STEPS - 1 - i, backward_window(STEPS - 1 - i))
+
+        @pl.when(i == STEPS // 2 + 1)
+        def _():
+            for c in reduce_z:
+                c.wait()
+            sb[...] = jnp.sum(ra[...], axis=0).reshape(sb.shape)
+            for c in reduce_y:
+                c.start()
+
+        @pl.when(i == STEPS // 2 + 4)
+        def _():
+            wait_sum(reduce_y, rb, br)
+            part = jnp.sum(rb[...], axis=0)
+            for n in range(NX):
+                sc[n] = part[2 * n : 2 * n + 2]
+            for c in reduce_x:
+                c.start()
+
+    wait_sum(reduce_x, rc, cr)
     gfilt[...] = jnp.sum(rc[...], axis=0)
 
     @pl.loop(0, STEPS)
@@ -383,15 +476,16 @@
         scratch_shapes=[
             *[pltpu.VMEM(slab, BF16)] * 8,
             pltpu.VMEM(into.shape, BF16), pltpu.VMEM(back.shape, BF16), pltpu.VMEM(tap.shape, BF16),
-            pltpu.VMEM((NX, 2, groups), F32), pltpu.VMEM((NYL, NZ, 2 * NX, groups), F32),
+            pltpu.VMEM((NX, 2, groups), F32), pltpu.VMEM((NYL, NZ, 16, TAPS), BF16),
             pltpu.VMEM((groups, WINDOW), F32), pltpu.VMEM((groups, WINDOW), F32),
+            pltpu.VMEM((rows // 2, WINDOW), F32), pltpu.VMEM((rows // 2, WINDOW), F32),
             pltpu.VMEM((NZ, 16, groups), F32), pltpu.VMEM((NZ, 16, groups), F32),
             pltpu.VMEM((NYL, 8, groups), F32), pltpu.VMEM((NY, 8, groups), F32),
             pltpu.VMEM((NX, 2, groups), F32), pltpu.VMEM((NX, 2, groups), F32),
             dma((4, LOADS)), dma((4,)), dma((2, STEPS)), dma((2, STEPS)),
-            dma((NX - 1,)), dma((NX - 1,)), dma((NZ - 1,)), dma((NZ - 1,)), dma, dma,
-            dma((NZ - 1,)), dma((NZ - 1,)), dma((NY - 1,)), dma((NY - 1,)),
-            dma((NX - 1,)), dma((NX - 1,)),
+            dma((NX - 1,)), dma((NX - 1,)), dma((2, NZ - 1)), dma((NZ - 1,)), dma((2,)), dma,
+            dma((NZ - 1,)), dma((NZ - 1,)), dma((NY,)), dma((NY,)),
+            dma((NX,)), dma((NX,)),
         ],
         compiler_params=pltpu.CompilerParams(
             collective_id=0, has_side_effects=True, vmem_limit_bytes=40 * 2**20

time: 66.1 us -> 45.1 us (0.68)
  Pallas kernels: 65.3 us -> 44.4 us
    pallas_call x1, Pallas kernels: 63.3 us -> 42.3 us  [local(): pl.pallas_call(mixer_kernel, out_shape=[pltpu.VMEM(slab, BF16)] * 4 + [pl...]
where the time goes in v2:
time: 45.1 us; the launch traced here: 45 us
  Pallas kernels  44.4 us (98%)
  between operations  0.64 us (1%)
    pallas_call x1, Pallas kernels, local(): pl.pallas_call(mixer_kernel, out_shape=[pltpu.VMEM(slab, BF16)] * 4 + [pl...  42.3 us
    pallas_call x1, Pallas kernels, local(): pl.pallas_call(write_kernel, out_shape=[pltpu.HBM(a.shape, a.dtype) for a...  2.05 us

profile of v2, /device:TPU:1, one launch (start us, length us, event | category | flops | bytes accessed | tf_op | source)
XLA Modules:
  0.0 45.0 jit_solution(11243828490310672816)
XLA Ops:
  0.6 42.3 %mixer.1 = (bf16[4096,128]{1,0:T(8,128)(2,1)S(1)}, bf16[4096,128]{1,0:T(8,128)(2,1)S(1)}, bf16[4096,128]{1,0:T(8,128)(2,1)S(1)}, bf16[4096,128]{1,0:T(8,128)(2,1)S(1)}, f32[2,256]{1,0:T(2,128)S(1)}) custom-call(bf16[4096,128]{1,0:T(8,128)(2,1)} %bitcast.10, bf16[4096,128]{1,0:T(8,128)(2,1)} %bitcast.11, bf16[4096,128]{1,0:T(8,128)(2,1)} %bitcast.12, ...), custom_call_target="tpu_custom_call" | custom-call | tf_op jit(solution)/shard_map/mixer/pallas_call | solution.py:471
  43.0 2.1 %write.1 = (bf16[4096,128]{1,0:T(8,128)(2,1)}, bf16[4096,128]{1,0:T(8,128)(2,1)}, bf16[4096,128]{1,0:T(8,128)(2,1)}, bf16[4096,128]{1,0:T(8,128)(2,1)}, f32[2,256]{1,0:T(2,128)}) custom-call(bf16[4096,128]{1,0:T(8,128)(2,1)S(1)} %get-tuple-element.15.refs_0_, bf16[4096,128]{1,0:T(8,128)(2,1)S(1)} %get-tuple-element.16.refs_1_, ...), custom_call_target="tpu_custom_call" | custom-call | tf_op jit(solution)/shard_map/write/pallas_call | solution.py:496

commit v3 on v2

--- a/solution.py
+++ b/solution.py
@@ -53,6 +53,10 @@
     return high, low
 
 
+def wrap(value, size):
+    return value - jnp.where(value >= size, size, 0)
+
+
 def mixer_kernel(
     q_h, k_h, v_h, go_h, f_h, into_h, back_h, tap_h,
     mixed, gq, gk, gv, gfilt,
@@ -70,19 +74,19 @@
     y = lax.div(dp, 2) * 4 + yl * 2 + lax.rem(dp, 2)
 
     def x_peer(d):
-        other = lax.rem(x + d, NX)
+        other = wrap(x + d, NX)
         return other, {"ctx": ctx - x + other}
 
     def z_peer(d):
-        other = lax.rem(z + d, NZ)
+        other = wrap(z + d, NZ)
         return other, {"ctx": ctx + (other - z) * NX}
 
     def beside_peer(d):
-        other = lax.rem(z + d, NZ)
+        other = wrap(z + d, NZ)
         return {"ctx": ctx + (other - z) * NX + 1 - 2 * lax.rem(x, 2)}
 
-    right = {"ctx": lax.rem(ctx + 1, last + 1)}
-    left = {"ctx": lax.rem(ctx + last, last + 1)}
+    right = {"ctx": wrap(ctx + 1, last + 1)}
+    left = {"ctx": wrap(ctx + last, last + 1)}
     half = NX * NZ
     other_half = {"ctx": ctx + (1 - 2 * yl) * half}
     unable = (ctx == 0) | (ctx == last)
@@ -93,7 +97,7 @@
     aside = 1 - 2 * lax.div(x, 2)
 
     def turn_z(amount):
-        return lax.rem(z + amount + NZ, NZ)
+        return wrap(wrap(z + amount + NZ, NZ), NZ)
 
     def sum_y_peer(t, amount):
         its_yl = (t // 2) % 2
@@ -109,6 +113,28 @@
         src, dst = ((k_h, k), (v_h, v), (q_h, q), (go_h, go))[which]
         at = pl.ds(pl.multiple_of(i * lrows, lrows), lrows)
         return pltpu.make_async_copy(src.at[at], dst.at[at], load_sem.at[which, i])
+
+    barrier = pltpu.get_barrier_semaphore()
+    middle = (x == 1) | (x == 2)
+    greeted = [sum_y_peer(t, -aside)[1] for t in range(NY)] + [right, left]
+    greeted += [x_peer(d)[1] for d in range(1, NX)]
+    greeted += [z_peer(d)[1] for d in range(1, NZ)]
+    greeted += [sum_x_peer(t, 2 * (t // 2) - 1) for t in range(NX)]
+    for device in greeted:
+        pl.semaphore_signal(barrier, inc=1, device_id=device, device_id_type=MESH)
+
+    @pl.when(jnp.logical_not(middle))
+    def _():
+        for d in range(1, NZ):
+            pl.semaphore_signal(barrier, inc=1, device_id=beside_peer(d), device_id_type=MESH)
+
+    @pl.when(jnp.logical_not(helped))
+    def _():
+        pl.semaphore_signal(barrier, inc=1, device_id=other_half, device_id_type=MESH)
+
+    @pl.when(helped)
+    def _():
+        pl.semaphore_signal(barrier, inc=1, device_id=helper_pair, device_id_type=MESH)
 
     taps_load = pltpu.make_async_copy(f_h, xg.at[x], const_sem.at[0])
     taps_load.start()
@@ -123,29 +149,6 @@
     ]
     for c in consts:
         c.start()
-
-    barrier = pltpu.get_barrier_semaphore()
-    middle = (x == 1) | (x == 2)
-    greeted = [right, left]
-    greeted += [x_peer(d)[1] for d in range(1, NX)]
-    greeted += [z_peer(d)[1] for d in range(1, NZ)]
-    greeted += [sum_y_peer(t, -aside)[1] for t in range(NY)]
-    greeted += [sum_x_peer(t, 2 * (t // 2) - 1) for t in range(NX)]
-    for device in greeted:
-        pl.semaphore_signal(barrier, inc=1, device_id=device, device_id_type=MESH)
-
-    @pl.when(jnp.logical_not(middle))
-    def _():
-        for d in range(1, NZ):
-            pl.semaphore_signal(barrier, inc=1, device_id=beside_peer(d), device_id_type=MESH)
-
-    @pl.when(jnp.logical_not(helped))
-    def _():
-        pl.semaphore_signal(barrier, inc=1, device_id=other_half, device_id_type=MESH)
-
-    @pl.when(helped)
-    def _():
-        pl.semaphore_signal(barrier, inc=1, device_id=helper_pair, device_id_type=MESH)
 
     def at_step(i):
         return pl.ds(pl.multiple_of(i * srows, srows), srows)
@@ -211,7 +214,7 @@
         other, device = z_peer(d)
         reduce_z.append(
             pltpu.make_async_remote_copy(
-                src_ref=sa.at[lax.rem(other + 2 * aside + NZ, NZ)], dst_ref=ra.at[z],
+                src_ref=sa.at[wrap(other + 2 * aside + jnp.where(aside < 0, NZ, 0), NZ)], dst_ref=ra.at[z],
                 send_sem=as_.at[d - 1], recv_sem=ar.at[d - 1],
                 device_id=device, device_id_type=MESH,
             )
@@ -246,26 +249,35 @@
     for c in gather_x:
         c.start()
 
+    paced_p, paced_gf = (x == NX - 1) & (ctx < last), (x == 0) & (ctx > 0)
+
     def send(n):
-        @pl.when(ctx < last)
+        @pl.when(paced_p)
         def _():
             send_p(n).start()
 
-        @pl.when(ctx > 0)
+        @pl.when(paced_gf)
         def _():
             send_gf(STEPS - 1 - n).start()
 
-    for s in range(per_load):
-        send(s)
+    def send_first(i):
+        for n in range(per_load):
+            n = i * per_load + n
+
+            @pl.when((ctx < last) & ((x < NX - 1) | (n < AHEAD)))
+            def _():
+                send_p(n).start()
+
+            @pl.when((ctx > 0) & ((x > 0) | (n < AHEAD)))
+            def _():
+                send_gf(STEPS - 1 - n).start()
+
+    send_first(0)
 
     @pl.loop(1, LOADS)
     def _(i):
         products(i)
-
-        @pl.when(i * per_load < AHEAD)
-        def _():
-            for s in range(per_load):
-                send(i * per_load + s)
+        send_first(i)
 
     @pl.when(ctx == 0)
     def _():
@@ -375,7 +387,7 @@
         tap[...], jnp.concatenate([high, high, low], axis=1),
         (((1,), (1,)), ((), ())), preferred_element_type=F32,
     )
-    sa[...] = grads.reshape(sa.shape)
+    sa[...] = grads.astype(BF16).reshape(sa.shape)
     ra[z] = sa[turn_z(2 * aside)]
     for c in reduce_z:
         c.start()
@@ -419,7 +431,7 @@
         def _():
             for c in reduce_z:
                 c.wait()
-            sb[...] = jnp.sum(ra[...], axis=0).reshape(sb.shape)
+            sb[...] = jnp.sum(ra[...].astype(F32), axis=0).reshape(sb.shape)
             for c in reduce_y:
                 c.start()
 
@@ -479,7 +491,7 @@
             pltpu.VMEM((NX, 2, groups), F32), pltpu.VMEM((NYL, NZ, 16, TAPS), BF16),
             pltpu.VMEM((groups, WINDOW), F32), pltpu.VMEM((groups, WINDOW), F32),
             pltpu.VMEM((rows // 2, WINDOW), F32), pltpu.VMEM((rows // 2, WINDOW), F32),
-            pltpu.VMEM((NZ, 16, groups), F32), pltpu.VMEM((NZ, 16, groups), F32),
+            pltpu.VMEM((NZ, 16, groups), BF16), pltpu.VMEM((NZ, 16, groups), BF16),
             pltpu.VMEM((NYL, 8, groups), F32), pltpu.VMEM((NY, 8, groups), F32),
             pltpu.VMEM((NX, 2, groups), F32), pltpu.VMEM((NX, 2, groups), F32),
             dma((4, LOADS)), dma((4,)), dma((2, STEPS)), dma((2, STEPS)),

time: 45.1 us -> 44.3 us (0.982)
  Pallas kernels: 44.4 us -> 43.6 us
    pallas_call x1, Pallas kernels: 42.3 us -> 41.6 us  [local(): pl.pallas_call(mixer_kernel, out_shape=[pltpu.VMEM(slab, BF16)] * 4 + [pl...]
where the time goes in v3:
time: 44.3 us
  Pallas kernels  43.6 us (98%)
  between operations  0.64 us (1%)
    pallas_call x1, Pallas kernels, local(): pl.pallas_call(mixer_kernel, out_shape=[pltpu.VMEM(slab, BF16)] * 4 + [pl...  41.6 us
    pallas_call x1, Pallas kernels, local(): pl.pallas_call(write_kernel, out_shape=[pltpu.HBM(a.shape, a.dtype) for a...  2.05 us

profile of v3, /device:TPU:1, one launch (start us, length us, event | category | flops | bytes accessed | tf_op | source)
XLA Modules:
  0.0 44.3 jit_solution(2580815687400300142)
XLA Ops:
  0.6 41.6 %mixer.1 = (bf16[4096,128]{1,0:T(8,128)(2,1)S(1)}, bf16[4096,128]{1,0:T(8,128)(2,1)S(1)}, bf16[4096,128]{1,0:T(8,128)(2,1)S(1)}, bf16[4096,128]{1,0:T(8,128)(2,1)S(1)}, f32[2,256]{1,0:T(2,128)S(1)}) custom-call(bf16[4096,128]{1,0:T(8,128)(2,1)} %bitcast.10, bf16[4096,128]{1,0:T(8,128)(2,1)} %bitcast.11, bf16[4096,128]{1,0:T(8,128)(2,1)} %bitcast.12, ...), custom_call_target="tpu_custom_call" | custom-call | tf_op jit(solution)/shard_map/mixer/pallas_call | solution.py:483
  42.2 2.1 %write.1 = (bf16[4096,128]{1,0:T(8,128)(2,1)}, bf16[4096,128]{1,0:T(8,128)(2,1)}, bf16[4096,128]{1,0:T(8,128)(2,1)}, bf16[4096,128]{1,0:T(8,128)(2,1)}, f32[2,256]{1,0:T(2,128)}) custom-call(bf16[4096,128]{1,0:T(8,128)(2,1)S(1)} %get-tuple-element.15.refs_0_, bf16[4096,128]{1,0:T(8,128)(2,1)S(1)} %get-tuple-element.16.refs_1_, ...), custom_call_target="tpu_custom_call" | custom-call | tf_op jit(solution)/shard_map/write/pallas_call | solution.py:508
